TPU v7x, 32 devices: a whole 2x2x4 slice. The times are simulated.
32 devices in a mesh: groups: 2 (over x), lon: 16 (over z, y, core).
Axes of the slice: x: 2, y: 2, z: 4, core: 2. Of those that a mesh axis runs over, the one named last changes fastest.
Arguments:
- queries: bfloat16 [8192, 1024], P(('groups', 'lon')), parts along dimension 0, may hold values from -8 to 8
- key_tokens: bfloat16 [8192, 1024], P(('groups', 'lon')), parts along dimension 0, may hold values from -8 to 8
- value_tokens: bfloat16 [8192, 1024], P(('groups', 'lon')), parts along dimension 0, may hold values from -6 to 6
- grad_out: bfloat16 [8192, 1024], P(('groups', 'lon')), parts along dimension 0, may hold values from -6 to 6
- out_weight: bfloat16 [1024, 1024], replicated, may hold values from -3 to 3
- pattern: int32 [32, 3], replicated, may hold values from 0 to 31, as said below
- valid_rows: int32 [32], replicated, may hold values from 64 to 128, as said below
Outputs:
- layer_out: bfloat16 [8192, 1024], P(('groups', 'lon')), parts along dimension 0
- grad_queries: bfloat16 [8192, 1024], P(('groups', 'lon')), parts along dimension 0
- grad_keys: bfloat16 [8192, 1024], P(('groups', 'lon')), parts along dimension 0
- grad_values: bfloat16 [8192, 1024], P(('groups', 'lon')), parts along dimension 0
There are 2 independent parts, one for each index of `groups`. A program takes and returns all parts, laid end to end along the dimension named above; an argument that names none is the same for every part. Nothing has to cross between parts.
Inputs may be any that keep to these rules, and one draw needn't show every extreme that they name: `pattern`: block g lies in longitude strip g // 2 at latitude index g % 2. Row g names three key blocks: column 1 is g itself, column 0 a block of strip (g // 2 - 1) mod 16, column 2 a block of strip (g // 2 + 1) mod 16, each at a latitude index that differs from g's by at most one. The first valid_rows[g] tokens of block g are live, the others are padding.
All inputs are finite; a program needn't handle non-finite values.
Results may differ from a plain program's by a relative error of at most 0.028.
Values may be sent and summed in bfloat16 or wider, within the bound.
A program may use at most 128 MiB of HBM per device.

v0:
```python
import jax
import jax.numpy as jnp
from jax import lax
from jax.sharding import PartitionSpec as P

HEADS = 16
TILE = 128


def with_halo(cells, sides, width):
    for axis, dim in sides:
        count = lax.axis_size(axis)
        head = lax.slice_in_dim(cells, 0, width, axis=dim)
        tail = lax.slice_in_dim(cells, cells.shape[dim] - width, cells.shape[dim], axis=dim)
        cells = jnp.concatenate(
            [
                lax.ppermute(tail, axis, [(i, (i + 1) % count) for i in range(count)]),
                cells,
                lax.ppermute(head, axis, [((i + 1) % count, i) for i in range(count)]),
            ],
            axis=dim,
        )
    return cells


def passed_along(block, axis, distance):
    devices = range(lax.axis_size(axis))
    route = [((i - distance) % len(devices), i) for i in devices]
    return lax.ppermute(block, axis, route)


def split_heads(tensor):
    return tensor.reshape(tensor.shape[:-1] + (HEADS, tensor.shape[-1] // HEADS))


def live_rows(counts):
    return jnp.arange(TILE, dtype=jnp.int32)[None, :] < counts[:, None]


def per_device(queries, key_tokens, value_tokens, grad_out, out_weight, pattern, valid_rows):
    strip_count = lax.axis_size("lon")
    position = lax.axis_index("lon")
    row_count, features = queries.shape
    blocks = row_count // TILE
    score_scale = (features // HEADS) ** (-0.5)
    near_span = 3 * TILE
    strips = (position + jnp.arange(3, dtype=jnp.int32) - 1) % strip_count
    near_counts = jnp.stack(
        [
            lax.dynamic_slice_in_dim(valid_rows, strips[offset] * blocks, blocks, 0)
            for offset in range(3)
        ]
    )
    near_pattern = jnp.stack(
        [
            lax.dynamic_slice_in_dim(pattern, strips[offset] * blocks, blocks, 0)
            for offset in range(3)
        ]
    )
    near_live = live_rows(near_counts.reshape(-1)).reshape(3, blocks, TILE)
    own_live = near_live[1]
    root_counts = jnp.sqrt(near_counts[1].astype(jnp.float32))
    picked = jnp.arange(3, dtype=jnp.int32)[None, :] * blocks + near_pattern[1] % blocks
    key_value = jnp.stack((key_tokens, value_tokens))
    bordered = with_halo(key_value, (("lon", 1),), row_count)
    bordered = bordered.reshape(2, 3 * blocks, TILE, features)
    pooled = jnp.einsum(
        "gt,xgtd->xgd",
        own_live.astype(jnp.bfloat16),
        key_value.reshape(2, blocks, TILE, features),
        preferred_element_type=jnp.float32,
    )
    summary = (pooled / root_counts[None, :, None]).astype(jnp.bfloat16)
    summaries = lax.all_gather(summary, "lon", axis=1, tiled=True)
    far_keys = split_heads(summaries[0])
    far_values = split_heads(summaries[1])
    far_count = summaries.shape[1]
    near_pairs = bordered[:, picked].reshape(2, blocks, near_span, features)
    near_keys = split_heads(near_pairs[0])
    near_values = split_heads(near_pairs[1])
    near_mask = near_live.reshape(3 * blocks, TILE)[picked].reshape(blocks, near_span)
    query_heads = split_heads(queries.reshape(blocks, TILE, features))
    near_scores = (
        jnp.einsum("bthc,blhc->bhtl", query_heads, near_keys, preferred_element_type=jnp.float32)
        * score_scale
    )
    near_scores = jnp.where(near_mask[:, None, None, :], near_scores, -jnp.inf)
    far_scores = (
        jnp.einsum("bthc,shc->bhts", query_heads, far_keys, preferred_element_type=jnp.float32)
        * score_scale
    )
    row_top = jnp.maximum(jnp.max(near_scores, axis=-1), jnp.max(far_scores, axis=-1))
    total = jnp.sum(jnp.exp(near_scores - row_top[..., None]), axis=-1) + jnp.sum(
        jnp.exp(far_scores - row_top[..., None]), axis=-1
    )
    log_total = row_top + jnp.log(total)
    near_chances = jnp.exp(near_scores - log_total[..., None])
    far_chances = jnp.exp(far_scores - log_total[..., None])
    near_rounded = near_chances.astype(jnp.bfloat16)
    far_rounded = far_chances.astype(jnp.bfloat16)
    mixed_heads = jnp.einsum(
        "bhtl,blhc->bthc", near_rounded, near_values, preferred_element_type=jnp.float32
    )
    mixed_heads = mixed_heads + jnp.einsum(
        "bhts,shc->bthc", far_rounded, far_values, preferred_element_type=jnp.float32
    )
    attended = mixed_heads.astype(jnp.bfloat16)
    layer_out = jnp.dot(
        attended.reshape(row_count, features), out_weight, preferred_element_type=jnp.float32
    ).astype(jnp.bfloat16)
    grad_attended = lax.dot_general(
        grad_out, out_weight, (((1,), (1,)), ((), ())), preferred_element_type=jnp.float32
    ).astype(jnp.bfloat16)
    grad_heads = split_heads(grad_attended.reshape(blocks, TILE, features))
    row_delta = jnp.einsum(
        "bthc,bthc->bht", grad_heads, attended, preferred_element_type=jnp.float32
    )
    near_grad_chances = jnp.einsum(
        "bthc,blhc->bhtl", grad_heads, near_values, preferred_element_type=jnp.float32
    )
    far_grad_chances = jnp.einsum(
        "bthc,shc->bhts", grad_heads, far_values, preferred_element_type=jnp.float32
    )
    near_grad_scores = (
        near_chances * (near_grad_chances - row_delta[..., None]) * score_scale
    ).astype(jnp.bfloat16)
    far_grad_scores = (
        far_chances * (far_grad_chances - row_delta[..., None]) * score_scale
    ).astype(jnp.bfloat16)
    grad_query = jnp.einsum(
        "bhtl,blhc->bthc", near_grad_scores, near_keys, preferred_element_type=jnp.float32
    )
    grad_query = grad_query + jnp.einsum(
        "bhts,shc->bthc", far_grad_scores, far_keys, preferred_element_type=jnp.float32
    )
    grad_queries = grad_query.astype(jnp.bfloat16).reshape(row_count, features)
    far_grad_keys = jnp.einsum(
        "bhts,bthc->shc", far_grad_scores, query_heads, preferred_element_type=jnp.float32
    ).reshape(far_count, features)
    far_grad_values = jnp.einsum(
        "bhts,bthc->shc", far_rounded, grad_heads, preferred_element_type=jnp.float32
    ).reshape(far_count, features)
    far_grads = lax.psum_scatter(
        jnp.stack((far_grad_keys, far_grad_values)), "lon", scatter_dimension=1, tiled=True
    )
    spread = (
        own_live.astype(jnp.float32)[None, :, :, None]
        * (far_grads / root_counts[None, :, None])[:, :, None, :]
    )
    spread = spread.reshape(2, row_count, features)
    near_grad_keys = jnp.einsum(
        "bhtl,bthc->blhc", near_grad_scores, query_heads, preferred_element_type=jnp.float32
    )
    near_grad_values = jnp.einsum(
        "bhtl,bthc->blhc", near_rounded, grad_heads, preferred_element_type=jnp.float32
    )
    onehot = (
        picked.reshape(-1)[:, None] == jnp.arange(3 * blocks, dtype=jnp.int32)[None, :]
    ).astype(jnp.float32)
    stacked = jnp.stack((near_grad_keys, near_grad_values)).reshape(2, 3 * blocks, TILE * features)
    placed = jnp.einsum("ne,xnk->xek", onehot, stacked, precision=lax.Precision.HIGHEST).reshape(
        2, 3, row_count, features
    )
    from_east = passed_along(placed[:, 0].astype(jnp.bfloat16), "lon", -1).astype(jnp.float32)
    from_west = passed_along(placed[:, 2].astype(jnp.bfloat16), "lon", 1).astype(jnp.float32)
    gathered = placed[:, 1] + from_east + from_west
    totals = gathered + spread
    return (layer_out, grad_queries, totals[0].astype(jnp.bfloat16), totals[1].astype(jnp.bfloat16))


def solution(mesh):
    return jax.shard_map(
        per_device,
        mesh=mesh,
        in_specs=(
            P(("groups", "lon"), None),
            P(("groups", "lon"), None),
            P(("groups", "lon"), None),
            P(("groups", "lon"), None),
            P(),
            P(),
            P(),
        ),
        out_specs=(
            P(("groups", "lon"), None),
            P(("groups", "lon"), None),
            P(("groups", "lon"), None),
            P(("groups", "lon"), None),
        ),
        check_vma=False,
    )
```

profile of v0, /device:TPU:0, one launch (start us, length us, event | category | flops | bytes accessed | tf_op | source)
XLA Modules:
  0.0 214.0 jit_solution(10437834198670715514)
XLA Ops:
  9.7 5.4 %collective-permute-start.1 = (bf16[2,256,1024]{2,1,0:T(8,128)(2,1)}, bf16[2,256,1024]{2,1,0:T(8,128)(2,1)}, u32[]{:S(2)}, u32[]{:S(2)}) collective-permute-start(bf16[2,256,1024]{2,1,0:T(8,128)(2,1)} %pad_maximum_fusion.1), channel_id=1, source_target_pairs={{1,0},{2,1},{3,2},{4,3},{5,4},{6,5},{7,6},{8,7},{9,8},{10,9},{11,1... | collective-permute-start | bytes 3145736 | tf_op jit(solution)/shard_map/ppermute | solution.py:19
  23.8 25.8 %all_gather.3 = bf16[2,32,1024]{2,0,1:T(2,128)(2,1)S(1)} all-gather(bf16[2,2,1024]{2,0,1:T(2,128)(2,1)S(1)} %fusion.47), channel_id=1, replica_groups=mesh['groups'=2,'lon'=16] {'lon'}, dimensions={1}, use_global_device_ids=true | all-gather | bytes 139264 | tf_op jit(solution)/shard_map/all_gather | solution.py:74
  50.8 2.6 %convolution_convert_fusion = bf16[256,1024]{1,0:T(8,128)(2,1)} fusion(bf16[256,1024]{1,0:T(8,128)(2,1)} %param.10, bf16[1024,1024]{1,0:T(8,128)(2,1)S(1)} %copy-done), kind=kOutput, calls=%fused_computation.30 | convolution fusion | flops 537133056 | bytes 3145728 | tf_op jit(solution)/shard_map/dot_general | solution.py:111
  59.5 3.4 %pad_maximum_fusion = bf16[2,768,1024]{2,1,0:T(8,128)(2,1)} fusion(bf16[2,256,1024]{2,1,0:T(8,128)(2,1)} %collective-permute-done.1, bf16[1,256,1024]{2,1,0:T(8,128)(2,1)} %bitcast.171, bf16[1,256,1024]{2,1,0:T(8,128)(2,1)} %bitcast.174, bf16[2,256,1024]{2,1,0:T(8,128)(2,1)} %collective-permute-done), kind=kLoop, calls=%fused_computation.15 | loop fusion | flops 12582912 | bytes 6291456 | tf_op jit(solution)/shard_map/concatenate | solution.py:15
  62.9 4.4 %gather_fusion = bf16[6,2,128,1024]{3,2,1,0:T(8,128)(2,1)} fusion(bf16[2,6,128,1024]{3,2,1,0:T(8,128)(2,1)} %bitcast.168, s32[1024]{0:T(1024)S(1)} %pad_clamp_fusion), kind=kCustom, calls=%fused_computation | custom fusion | bytes 6291480 | tf_op jit(solution)/shard_map/gather | solution.py:78
  67.3 3.8 %fusion.62 = (bf16[1,2,3,128,1024]{4,3,0,2,1:T(8,128)(2,1)}, bf16[1,2,3,128,1024]{4,3,0,2,1:T(8,128)(2,1)}) fusion(bf16[2,2,3,128,1024]{4,3,0,2,1:T(8,128)(2,1)} %bitcast.167), kind=kLoop, calls=%fused_computation.116 | loop fusion | bytes 6291456 | tf_op jit(solution)/shard_map/slice | solution.py:80
  71.1 4.2 %copy.108 = bf16[1,2,3,128,1024]{3,2,4,1,0:T(4,128)(2,1)} copy(bf16[1,2,3,128,1024]{4,3,0,2,1:T(8,128)(2,1)} %get-tuple-element.22) | data formatting | bytes 3145728 | tf_op jit(solution)/shard_map/slice | solution.py:80
  75.3 5.1 %reshape_squeeze.12 = bf16[2,384,16,64]{1,3,2,0:T(8,128)(2,1)} reshape(bf16[1,2,3,128,1024]{3,2,4,1,0:T(4,128)(2,1)} %copy.108) | data formatting | bytes 3145728 | tf_op jit(solution)/shard_map/reshape;squeeze | solution.py:33
  80.4 4.2 %copy.109 = bf16[1,2,3,128,1024]{3,2,4,1,0:T(4,128)(2,1)} copy(bf16[1,2,3,128,1024]{4,3,0,2,1:T(8,128)(2,1)} %get-tuple-element.23) | data formatting | bytes 3145728 | tf_op jit(solution)/shard_map/slice | solution.py:79
  84.6 5.1 %reshape_squeeze.13 = bf16[2,384,16,64]{1,3,2,0:T(8,128)(2,1)} reshape(bf16[1,2,3,128,1024]{3,2,4,1,0:T(4,128)(2,1)} %copy.109) | data formatting | bytes 3145728 | tf_op jit(solution)/shard_map/reshape;squeeze | solution.py:33
  89.7 3.0 %bitcast_reduce_fusion = (f32[2,16,128]{2,1,0:T(8,128)S(1)}, f32[2,16,384,128]{3,2,1,0:T(8,128)S(1)}) fusion(pred[2,384]{1,0:T(4,128)(4,1)S(1)} %broadcast_in_dim.17, bf16[2,384,16,64]{1,3,2,0:T(8,128)(2,1)} %reshape_squeeze.13, bf16[2,128,16,64]{1,0,3,2:T(2,128)(2,1)S(1)} %reshape_reshape.6), kind=kOutput, calls=%fused_computation.8 | convolution fusion | flops 206041088 | bytes 8405760 | tf_op jit(solution)/shard_map/bthc,blhc->bhtl/dot_general | solution.py:84
  95.9 2.6 %multiply_reduce_fusion = (f32[2,16,128]{2,1,0:T(8,128)S(1)}, bf16[2,128,16,64]{1,3,2,0:T(8,128)(2,1)}) fusion(f32[2,16,128,64]{2,0,3,1:T(2,128)S(1)} %copy-done.7, f32[2,128,16,64]{1,3,2,0:T(8,128)S(1)} %convolution_bitcast_fusion.4, bf16[2,384,16,64]{1,3,2,0:T(8,128)(2,1)S(1)} %copy-done.5, f32[2,16,384,128]{3,2,1,0:T(8,128)S(1)} %get-tuple-element.35, ...), kind=kOutput, calls=%fused_computation.47 | convolution fusion | flops 208924672 | bytes 10519296 | tf_op jit(solution)/shard_map/bhtl,blhc->bthc/dot_general | solution.py:101
  99.1 3.9 %multiply_convert_fusion = bf16[2,16,128,384]{2,3,1,0:T(8,128)(2,1)} fusion(f32[2,16,384,128]{3,2,1,0:T(8,128)S(1)} %get-tuple-element.35, f32[2,16,128]{2,1,0:T(8,128)S(1)} %get-tuple-element.38, f32[2,16,128]{2,1,0:T(8,128)S(1)} %fusion.45, pred[2,384]{1,0:T(4,128)(4,1)S(1)} %broadcast_in_dim.17, bf16[2,384,16,64]{1,3,2,0:T(8,128)(2,1)S(1)} %copy-done.5, ...), kind=kOutput, calls=%fused_computation.12 | convolution fusion | flops 212336640 | bytes 11567872 | tf_op jit(solution)/shard_map/bthc,blhc->bhtl/dot_general | solution.py:118
  103.0 3.2 %convolution_bitcast_fusion.1 = f32[2,384,16,64]{1,3,2,0:T(8,128)} fusion(bf16[2,128,16,64]{1,0,3,2:T(2,128)(2,1)S(1)} %copy-done.2, f32[2,16,384,128]{3,2,1,0:T(8,128)S(1)} %get-tuple-element.35, f32[2,16,128]{2,1,0:T(8,128)S(1)} %fusion.45, pred[2,384]{1,0:T(4,128)(4,1)S(1)} %broadcast_in_dim.17), kind=kOutput, calls=%fused_computation.22 | convolution fusion | flops 207618048 | bytes 9978624 | tf_op jit(solution)/shard_map/bhtl,bthc->blhc/dot_general | solution.py:154
  113.1 5.1 %convolution_bitcast_fusion.2 = f32[2,384,16,64]{1,3,2,0:T(8,128)} fusion(bf16[2,16,128,384]{2,3,1,0:T(8,128)(2,1)} %multiply_convert_fusion, bf16[2,128,16,64]{1,0,3,2:T(2,128)(2,1)S(1)} %reshape_reshape.6), kind=kOutput, calls=%fused_computation.23 | convolution fusion | flops 201326592 | bytes 6815744 | tf_op jit(solution)/shard_map/bhtl,bthc->blhc/dot_general | solution.py:151
  118.2 6.1 %copy.134 = f32[2,384,16,64]{3,2,1,0:T(8,128)} copy(f32[2,384,16,64]{1,3,2,0:T(8,128)} %convolution_bitcast_fusion.2) | data formatting | bytes 6291456 | tf_op jit(solution)/shard_map/bhtl,bthc->blhc/transpose | solution.py:151
  124.3 6.6 %stack.49 = f32[1,6,131072]{2,1,0:T(8,128)} reshape(f32[2,384,16,64]{3,2,1,0:T(8,128)} %copy.134) | data formatting | bytes 6291456 | tf_op jit(solution)/shard_map/stack | solution.py:160
  130.9 6.1 %copy.137 = f32[2,384,16,64]{3,2,1,0:T(8,128)} copy(f32[2,384,16,64]{1,3,2,0:T(8,128)} %convolution_bitcast_fusion.1) | data formatting | bytes 6291456 | tf_op jit(solution)/shard_map/bhtl,bthc->blhc/transpose | solution.py:154
  137.0 6.6 %stack.50 = f32[1,6,131072]{2,1,0:T(8,128)} reshape(f32[2,384,16,64]{3,2,1,0:T(8,128)} %copy.137) | data formatting | bytes 6291456 | tf_op jit(solution)/shard_map/stack | solution.py:160
  143.7 11.1 %convolution_bitcast_fusion = f32[2,6,131072]{2,1,0:T(8,128)} fusion(f32[1,6,131072]{2,1,0:T(8,128)} %stack.50, f32[1,6,131072]{2,1,0:T(8,128)} %stack.49, s32[6]{0:T(128)S(1)} %copy-done.12), kind=kOutput, calls=%fused_computation.2 | convolution fusion | flops 114819104 | bytes 12582936 | tf_op jit(solution)/shard_map/ne,xnk->xek/dot_general | solution.py:161
  154.8 7.2 %reshape.84 = f32[2,3,256,1024]{3,2,1,0:T(8,128)} reshape(f32[2,6,131072]{2,1,0:T(8,128)} %convolution_bitcast_fusion) | data formatting | bytes 12582912 | tf_op jit(solution)/shard_map/reshape | solution.py:161
  161.9 3.3 %convert.9 = bf16[2,3,256,1024]{3,2,1,0:T(8,128)(2,1)S(1)} convert(f32[2,3,256,1024]{3,2,1,0:T(8,128)} %reshape.84) | non-fusion elementwise | flops 1572864 | bytes 9437184 | tf_op jit(solution)/shard_map/convert.4
  175.0 27.4 %all-reduce.3.cloned.1.call-done = f32[2,32,1024]{2,1,0:T(8,128)} async-done(((f32[2,32,1024]{2,1,0:T(8,128)}), f32[2,32,1024]{2,1,0:T(8,128)}) %all-reduce.3.cloned.1.call-update) | async-done | bytes 262160
  203.3 2.8 %fusion.10 = bf16[2,256,1024]{2,1,0:T(8,128)(2,1)S(1)} fusion(f32[2,3,256,1024]{3,2,1,0:T(8,128)} %reshape.84, bf16[2,256,1024]{2,1,0:T(8,128)(2,1)} %collective-permute-done.3, bf16[2,256,1024]{2,1,0:T(8,128)(2,1)} %collective-permute-done.2, f32[2,2,1024]{2,1,0:T(2,128)S(1)} %dynamic-slice_divide_fusion, f32[256]{0:T(256)S(1)} %copy-done.9), kind=kLoop, calls=%fused_computation.20 | loop fusion | flops 3670016 | bytes 5260288 | tf_op jit(solution)/shard_map/convert.2
  (92 shorter events, 38.0 us)
Async XLA Ops:
  7.2 43.6 %copy-start = (bf16[1024,1024]{1,0:T(8,128)(2,1)S(1)}, bf16[1024,1024]{1,0:T(8,128)(2,1)}, u32[]{:S(2)}) copy-start(bf16[1024,1024]{1,0:T(8,128)(2,1)} %param.11) | copy-start | bytes 6291460
  7.2 43.3 %copy-start.8 = (bf16[256,1024]{1,0:T(8,128)(2,1)S(1)}, bf16[256,1024]{1,0:T(8,128)(2,1)}, u32[]{:S(2)}) copy-start(bf16[256,1024]{1,0:T(8,128)(2,1)} %param.7) | copy-start | bytes 1572868
  7.2 195.2 %all-reduce.3.cloned.1.call-start = ((), (), s32[]{:S(2)}) async-start(), calls=%async_computation | async-start | bytes 524288
  9.7 49.8 %collective-permute-start.1 = (bf16[2,256,1024]{2,1,0:T(8,128)(2,1)}, bf16[2,256,1024]{2,1,0:T(8,128)(2,1)}, u32[]{:S(2)}, u32[]{:S(2)}) collective-permute-start(bf16[2,256,1024]{2,1,0:T(8,128)(2,1)} %pad_maximum_fusion.1), channel_id=1, source_target_pairs={{1,0},{2,1},{3,2},{4,3},{5,4},{6,5},{7,6},{8,7},{9,8},{10,9},{11,1... | collective-permute-start | bytes 3145736 | tf_op jit(solution)/shard_map/ppermute | solution.py:19
  15.1 44.3 %collective-permute-start = (bf16[2,256,1024]{2,1,0:T(8,128)(2,1)}, bf16[2,256,1024]{2,1,0:T(8,128)(2,1)}, u32[]{:S(2)}, u32[]{:S(2)}) collective-permute-start(bf16[2,256,1024]{2,1,0:T(8,128)(2,1)} %pad_maximum_fusion.1), channel_id=1, source_target_pairs={{0,1},{1,2},{2,3},{3,4},{4,5},{5,6},{6,7},{7,8},{8,9},{9,10},{10,1... | collective-permute-start | bytes 3145736 | tf_op jit(solution)/shard_map/ppermute | solution.py:17
  18.4 5.4 %copy-start.10 = (f32[2]{0:T(128)}, f32[2]{0:T(128)S(1)}, u32[]{:S(2)}) copy-start(f32[2]{0:T(128)S(1)} %convert_sqrt_fusion) | copy-start | bytes 28
  50.3 44.4 %copy-start.6 = (bf16[32,16,64]{2,1,0:T(8,128)(2,1)}, bf16[32,16,64]{2,1,0:T(8,128)(2,1)S(1)}, u32[]{:S(2)}) copy-start(bf16[32,16,64]{2,1,0:T(8,128)(2,1)S(1)} %reshape_squeeze.15) | copy-start | bytes 196612
  50.6 4.9 %copy-start.13 = (u32[32]{0:T(128)S(1)}, u32[32]{0:T(128)}, u32[]{:S(2)}) copy-start(u32[32]{0:T(128)} %constant.57) | copy-start | bytes 388
  92.7 1.6 copy-start.2
  94.2 1.4 copy-start.5
  94.2 1.7 copy-start.7
  137.0 6.6 %copy-start.12 = (s32[6]{0:T(128)S(1)}, s32[6]{0:T(128)}, u32[]{:S(2)}) copy-start(s32[6]{0:T(128)} %eq.19) | copy-start | bytes 76
  165.2 3.3 %copy-start.1 = (bf16[2,384,16,64]{1,3,2,0:T(8,128)(2,1)S(1)}, bf16[2,384,16,64]{1,3,2,0:T(8,128)(2,1)}, u32[]{:S(2)}) copy-start(bf16[2,384,16,64]{1,3,2,0:T(8,128)(2,1)} %reshape_squeeze.13) | copy-start | bytes 4718596
  165.2 3.3 %copy-start.3 = (bf16[2,16,128,384]{2,3,1,0:T(8,128)(2,1)S(1)}, bf16[2,16,128,384]{2,3,1,0:T(8,128)(2,1)}, u32[]{:S(2)}) copy-start(bf16[2,16,128,384]{2,3,1,0:T(8,128)(2,1)} %multiply_convert_fusion) | copy-start | bytes 9437188
  166.7 36.6 %collective-permute-start.2 = (bf16[2,256,1024]{2,1,0:T(8,128)(2,1)}, bf16[2,256,1024]{2,1,0:T(8,128)(2,1)}, u32[]{:S(2)}, u32[]{:S(2)}) collective-permute-start(bf16[2,256,1024]{2,1,0:T(8,128)(2,1)} %get-tuple-element.20), channel_id=1, source_target_pairs={{1,0},{2,1},{3,2},{4,3},{5,4},{6,5},{7,6},{8,7},{9,8},{10,9},{11,1... | collective-permute-start | bytes 3145736 | tf_op jit(solution)/shard_map/ppermute | solution.py:29
  168.2 35.1 %collective-permute-start.3 = (bf16[2,256,1024]{2,1,0:T(8,128)(2,1)}, bf16[2,256,1024]{2,1,0:T(8,128)(2,1)}, u32[]{:S(2)}, u32[]{:S(2)}) collective-permute-start(bf16[2,256,1024]{2,1,0:T(8,128)(2,1)} %get-tuple-element.21), channel_id=1, source_target_pairs={{15,0},{0,1},{1,2},{2,3},{3,4},{4,5},{5,6},{6,7},{7,8},{8,9},{9,10... | collective-permute-start | bytes 3145736 | tf_op jit(solution)/shard_map/ppermute | solution.py:29
  168.5 1.6 copy-start.4
  170.1 32.3 %copy-start.11 = (f32[2]{0:T(128)S(1)}, f32[2]{0:T(128)}, u32[]{:S(2)}) copy-start(f32[2]{0:T(128)} %copy-done.10) | copy-start | bytes 28
  170.1 33.2 %copy-start.9 = (f32[256]{0:T(256)S(1)}, f32[256]{0:T(256)}, u32[]{:S(2)}) copy-start(f32[256]{0:T(256)} %get-tuple-element.26) | copy-start | bytes 3076
Sparse Core Ops, SparseCore 0:
  113.2 89.1 all-reduce.2
where the time goes:
time: 215 us; the launch traced here: 214 us
  local copies, waits for them, and re-layouts  77.4 us (36%)
  matrix products  38.8 us (18%)
  waiting for transfers between devices  27.4 us (13%)
  blocking collectives  25.8 us (12%)
  other arithmetic  20.7 us (10%)
  between operations  16.9 us (8%)
  starting transfers between devices  6.92 us (3%)
    unnamed x2, waiting for transfers between devices  27.4 us
    all_gather x1, blocking collectives, per_device(): summaries = lax.all_gather(summary, 'lon', axis=1, tiled=True)  25.8 us
    another operation x2, local copies, waits for them, and re-layouts, per_device(): jnp.stack((near_grad_keys, near_grad_values))  13.3 us
    another operation x6, local copies, waits for them, and re-layouts, split_heads(): tensor.reshape(tensor.shape[:-1] + (HEADS, tensor.shape[-1] // HEADS))  11.6 us
    dot_general x1, matrix products, per_device(): jnp.einsum('ne,xnk->xek', onehot, stacked, precision=lax.Precision.HIGHEST)  11.1 us
    slice x2, local copies, waits for them, and re-layouts, per_device(): near_values = split_heads(near_pairs[1])  7.98 us
    reshape x1, local copies, waits for them, and re-layouts, per_device(): jnp.einsum('ne,xnk->xek', onehot, stacked, precision=lax.Precision.HIGHEST)  7.16 us
    transpose x1, local copies, waits for them, and re-layouts, per_device(): jnp.einsum('bhtl,bthc->blhc', near_grad_scores, query_heads, preferred_el...  6.11 us
  transfers between devices with their start and end apart: 5, of which 1 were waited for; matrix products, arithmetic and copies ran while one was open for 36% of the time, Pallas kernels for 0%

commit v1 on v0

--- a/solution.py
+++ b/solution.py
@@ -5,6 +5,23 @@
 
 HEADS = 16
 TILE = 128
+
+
+def joined_along(blocks, dim):
+    blocks = jnp.moveaxis(blocks, 0, dim)
+    dims = blocks.shape
+    return blocks.reshape(*dims[:dim], dims[dim] * dims[dim + 1], *dims[dim + 2 :])
+
+
+def doubled(array, axis):
+    peers, index = (lax.axis_size(axis), lax.axis_index(axis))
+    blocks, stride = (array[None], 1)
+    while stride < peers:
+        other = lax.ppermute(blocks, axis, [(i, i ^ stride) for i in range(peers)])
+        low = index & stride == 0
+        blocks = jnp.concatenate([jnp.where(low, blocks, other), jnp.where(low, other, blocks)])
+        stride *= 2
+    return blocks
 
 
 def with_halo(cells, sides, width):
@@ -71,7 +88,7 @@
         preferred_element_type=jnp.float32,
     )
     summary = (pooled / root_counts[None, :, None]).astype(jnp.bfloat16)
-    summaries = lax.all_gather(summary, "lon", axis=1, tiled=True)
+    summaries = joined_along(doubled(summary, "lon"), 1)
     far_keys = split_heads(summaries[0])
     far_values = split_heads(summaries[1])
     far_count = summaries.shape[1]

time: 215 us -> 207 us (0.963)
  blocking collectives: 25.8 us -> 0 us
  waiting for transfers between devices: 27.4 us -> 41.9 us
  starting transfers between devices: 6.92 us -> 11.6 us
    all_gather x1 -> x0, blocking collectives: 25.8 us -> none  [per_device(): summaries = lax.all_gather(summary, 'lon', axis=1, tiled=True)]
    ppermute x0 -> x4, waiting for transfers between devices: none -> 14.2 us  [doubled(): other = lax.ppermute(blocks, axis, [(i, i ^ stride) for i in range(peers)])]
    ppermute x0 -> x4, starting transfers between devices: none -> 4.44 us  [doubled(): other = lax.ppermute(blocks, axis, [(i, i ^ stride) for i in range(peers)])]
    unnamed x32 -> x40, local copies, waits for them, and re-layouts: 5.05 us -> 6.91 us
  transfers between devices with their start and end apart: 5 -> 9, of which waited for: 1 -> 3; matrix products, arithmetic and copies ran while one was open for 36% -> 37% of each run, Pallas kernels for 0% -> 0%
where the time goes in v1:
time: 207 us; the launch traced here: 205 us
  local copies, waits for them, and re-layouts  78 us (38%)
  waiting for transfers between devices  41.9 us (20%)
  matrix products  37 us (18%)
  other arithmetic  19.8 us (10%)
  between operations  17.1 us (8%)
  starting transfers between devices  11.6 us (6%)
    unnamed x2, waiting for transfers between devices  27.7 us
    ppermute x4, waiting for transfers between devices, doubled(): other = lax.ppermute(blocks, axis, [(i, i ^ stride) for i in range(peers)])  14.2 us
    another operation x2, local copies, waits for them, and re-layouts, per_device(): jnp.stack((near_grad_keys, near_grad_values))  13.3 us
    another operation x6, local copies, waits for them, and re-layouts, split_heads(): tensor.reshape(tensor.shape[:-1] + (HEADS, tensor.shape[-1] // HEADS))  11.8 us
    dot_general x1, matrix products, per_device(): jnp.einsum('ne,xnk->xek', onehot, stacked, precision=lax.Precision.HIGHEST)  11.1 us
    slice x2, local copies, waits for them, and re-layouts, per_device(): near_values = split_heads(near_pairs[1])  8.02 us
    reshape x1, local copies, waits for them, and re-layouts, per_device(): jnp.einsum('ne,xnk->xek', onehot, stacked, precision=lax.Precision.HIGHEST)  7.17 us
    unnamed x40, local copies, waits for them, and re-layouts  6.91 us
  transfers between devices with their start and end apart: 9, of which 3 were waited for; matrix products, arithmetic and copies ran while one was open for 37% of the time, Pallas kernels for 0%

profile of v1, /device:TPU:0, one launch (start us, length us, event | category | flops | bytes accessed | tf_op | source)
XLA Modules:
  0.0 205.4 jit_solution(11455381619119806778)
XLA Ops:
  9.7 5.4 %collective-permute-start.1 = (bf16[2,256,1024]{2,1,0:T(8,128)(2,1)}, bf16[2,256,1024]{2,1,0:T(8,128)(2,1)}, u32[]{:S(2)}, u32[]{:S(2)}) collective-permute-start(bf16[2,256,1024]{2,1,0:T(8,128)(2,1)} %pad_maximum_fusion.1), channel_id=1, source_target_pairs={{1,0},{2,1},{3,2},{4,3},{5,4},{6,5},{7,6},{8,7},{9,8},{10,9},{11,1... | collective-permute-start | bytes 3145736 | tf_op jit(solution)/shard_map/ppermute | solution.py:36
  24.5 12.8 %collective-permute-done.3 = bf16[2,2,2,1024]{3,2,0,1:T(2,128)(2,1)S(1)} collective-permute-done((bf16[2,2,2,1024]{3,2,0,1:T(2,128)(2,1)S(1)}, bf16[2,2,2,1024]{3,2,0,1:T(2,128)(2,1)S(1)}, u32[]{:S(2)}, u32[]{:S(2)}) %collective-permute-start.3) | collective-permute-done | bytes 16416 | tf_op jit(solution)/shard_map/ppermute | solution.py:20
  41.5 2.7 %collective-permute-start.5 = (bf16[8,2,2,1024]{3,2,0,1:T(2,128)(2,1)S(1)}, bf16[8,2,2,1024]{3,2,0,1:T(2,128)(2,1)S(1)}, u32[]{:S(2)}, u32[]{:S(2)}) collective-permute-start(bf16[8,2,2,1024]{3,2,0,1:T(2,128)(2,1)S(1)} %pad_maximum_fusion.4), channel_id=1, source_target_pairs={{0,8},{1,9},{2,10},{3,11},{4,12},{5,13},{6,14},{7,15},{8,0},{9,1},... | collective-permute-start | bytes 196616 | tf_op jit(solution)/shard_map/ppermute | solution.py:20
  50.2 3.4 %pad_maximum_fusion = bf16[2,768,1024]{2,1,0:T(8,128)(2,1)} fusion(bf16[2,256,1024]{2,1,0:T(8,128)(2,1)} %collective-permute-done.1, bf16[1,256,1024]{2,1,0:T(8,128)(2,1)} %bitcast.179, bf16[1,256,1024]{2,1,0:T(8,128)(2,1)} %bitcast.182, bf16[2,256,1024]{2,1,0:T(8,128)(2,1)} %collective-permute-done), kind=kLoop, calls=%fused_computation.15 | loop fusion | flops 12582912 | bytes 6291456 | tf_op jit(solution)/shard_map/concatenate | solution.py:32
  53.6 4.4 %gather_fusion = bf16[6,2,128,1024]{3,2,1,0:T(8,128)(2,1)} fusion(bf16[2,6,128,1024]{3,2,1,0:T(8,128)(2,1)} %bitcast.176, s32[1024]{0:T(1024)S(1)} %pad_clamp_fusion), kind=kCustom, calls=%fused_computation | custom fusion | bytes 6291480 | tf_op jit(solution)/shard_map/gather | solution.py:95
  58.0 3.9 %fusion.62 = (bf16[1,2,3,128,1024]{4,3,0,2,1:T(8,128)(2,1)}, bf16[1,2,3,128,1024]{4,3,0,2,1:T(8,128)(2,1)}) fusion(bf16[2,2,3,128,1024]{4,3,0,2,1:T(8,128)(2,1)} %bitcast.175), kind=kLoop, calls=%fused_computation.126 | loop fusion | bytes 6291456 | tf_op jit(solution)/shard_map/slice | solution.py:97
  61.9 4.1 %copy.108 = bf16[1,2,3,128,1024]{3,2,4,1,0:T(4,128)(2,1)} copy(bf16[1,2,3,128,1024]{4,3,0,2,1:T(8,128)(2,1)} %get-tuple-element.20) | data formatting | bytes 3145728 | tf_op jit(solution)/shard_map/slice | solution.py:97
  66.1 5.1 %reshape_squeeze.12 = bf16[2,384,16,64]{1,3,2,0:T(8,128)(2,1)} reshape(bf16[1,2,3,128,1024]{3,2,4,1,0:T(4,128)(2,1)} %copy.108) | data formatting | bytes 3145728 | tf_op jit(solution)/shard_map/reshape;squeeze | solution.py:50
  71.2 4.1 %copy.109 = bf16[1,2,3,128,1024]{3,2,4,1,0:T(4,128)(2,1)} copy(bf16[1,2,3,128,1024]{4,3,0,2,1:T(8,128)(2,1)} %get-tuple-element.21) | data formatting | bytes 3145728 | tf_op jit(solution)/shard_map/slice | solution.py:96
  75.3 5.1 %reshape_squeeze.13 = bf16[2,384,16,64]{1,3,2,0:T(8,128)(2,1)} reshape(bf16[1,2,3,128,1024]{3,2,4,1,0:T(4,128)(2,1)} %copy.109) | data formatting | bytes 3145728 | tf_op jit(solution)/shard_map/reshape;squeeze | solution.py:50
  80.5 3.0 %bitcast_reduce_fusion = (f32[2,16,128]{2,1,0:T(8,128)S(1)}, f32[2,16,384,128]{3,2,1,0:T(8,128)S(1)}) fusion(pred[2,384]{1,0:T(4,128)(4,1)S(1)} %broadcast_in_dim.19, bf16[2,384,16,64]{1,3,2,0:T(8,128)(2,1)} %reshape_squeeze.13, bf16[2,128,16,64]{1,0,3,2:T(2,128)(2,1)S(1)} %reshape_reshape.6), kind=kOutput, calls=%fused_computation.8 | convolution fusion | flops 206041088 | bytes 8405760 | tf_op jit(solution)/shard_map/bthc,blhc->bhtl/dot_general | solution.py:101
  86.7 2.6 %multiply_reduce_fusion = (f32[2,16,128]{2,1,0:T(8,128)S(1)}, bf16[2,128,16,64]{1,3,2,0:T(8,128)(2,1)}) fusion(f32[2,16,128,64]{2,0,3,1:T(2,128)S(1)} %copy-done.8, f32[2,128,16,64]{1,3,2,0:T(8,128)S(1)} %convolution_bitcast_fusion.4, bf16[2,384,16,64]{1,3,2,0:T(8,128)(2,1)S(1)} %copy-done.6, f32[2,16,384,128]{3,2,1,0:T(8,128)S(1)} %get-tuple-element.43, ...), kind=kOutput, calls=%fused_computation.47 | convolution fusion | flops 208924672 | bytes 10519296 | tf_op jit(solution)/shard_map/bhtl,blhc->bthc/dot_general | solution.py:118
  89.9 3.9 %multiply_convert_fusion = bf16[2,16,128,384]{2,3,1,0:T(8,128)(2,1)} fusion(f32[2,16,384,128]{3,2,1,0:T(8,128)S(1)} %get-tuple-element.43, f32[2,16,128]{2,1,0:T(8,128)S(1)} %get-tuple-element.46, f32[2,16,128]{2,1,0:T(8,128)S(1)} %fusion.45, pred[2,384]{1,0:T(4,128)(4,1)S(1)} %copy-done.10, bf16[2,384,16,64]{1,3,2,0:T(8,128)(2,1)S(1)} %copy-done.6, ...), kind=kOutput, calls=%fused_computation.12 | convolution fusion | flops 212336640 | bytes 11567872 | tf_op jit(solution)/shard_map/bthc,blhc->bhtl/dot_general | solution.py:135
  93.8 3.2 %convolution_bitcast_fusion.1 = f32[2,384,16,64]{1,3,2,0:T(8,128)} fusion(bf16[2,128,16,64]{1,0,3,2:T(2,128)(2,1)S(1)} %copy-done.3, f32[2,16,384,128]{3,2,1,0:T(8,128)S(1)} %get-tuple-element.43, f32[2,16,128]{2,1,0:T(8,128)S(1)} %fusion.45, pred[2,384]{1,0:T(4,128)(4,1)S(1)} %copy-done.10), kind=kOutput, calls=%fused_computation.22 | convolution fusion | flops 207618048 | bytes 9978624 | tf_op jit(solution)/shard_map/bhtl,bthc->blhc/dot_general | solution.py:171
  103.9 5.1 %convolution_bitcast_fusion.2 = f32[2,384,16,64]{1,3,2,0:T(8,128)} fusion(bf16[2,16,128,384]{2,3,1,0:T(8,128)(2,1)} %multiply_convert_fusion, bf16[2,128,16,64]{1,0,3,2:T(2,128)(2,1)S(1)} %reshape_reshape.6), kind=kOutput, calls=%fused_computation.23 | convolution fusion | flops 201326592 | bytes 6815744 | tf_op jit(solution)/shard_map/bhtl,bthc->blhc/dot_general | solution.py:168
  109.0 6.1 %copy.134 = f32[2,384,16,64]{3,2,1,0:T(8,128)} copy(f32[2,384,16,64]{1,3,2,0:T(8,128)} %convolution_bitcast_fusion.2) | data formatting | bytes 6291456 | tf_op jit(solution)/shard_map/bhtl,bthc->blhc/transpose | solution.py:168
  115.1 6.7 %stack.49 = f32[1,6,131072]{2,1,0:T(8,128)} reshape(f32[2,384,16,64]{3,2,1,0:T(8,128)} %copy.134) | data formatting | bytes 6291456 | tf_op jit(solution)/shard_map/stack | solution.py:177
  121.8 6.1 %copy.137 = f32[2,384,16,64]{3,2,1,0:T(8,128)} copy(f32[2,384,16,64]{1,3,2,0:T(8,128)} %convolution_bitcast_fusion.1) | data formatting | bytes 6291456 | tf_op jit(solution)/shard_map/bhtl,bthc->blhc/transpose | solution.py:171
  127.9 6.6 %stack.50 = f32[1,6,131072]{2,1,0:T(8,128)} reshape(f32[2,384,16,64]{3,2,1,0:T(8,128)} %copy.137) | data formatting | bytes 6291456 | tf_op jit(solution)/shard_map/stack | solution.py:177
  134.5 11.1 %convolution_bitcast_fusion = f32[2,6,131072]{2,1,0:T(8,128)} fusion(f32[1,6,131072]{2,1,0:T(8,128)} %stack.50, f32[1,6,131072]{2,1,0:T(8,128)} %stack.49, s32[6]{0:T(128)S(1)} %copy-done.15), kind=kOutput, calls=%fused_computation.2 | convolution fusion | flops 114819104 | bytes 12582936 | tf_op jit(solution)/shard_map/ne,xnk->xek/dot_general | solution.py:178
  145.7 7.2 %reshape.89 = f32[2,3,256,1024]{3,2,1,0:T(8,128)} reshape(f32[2,6,131072]{2,1,0:T(8,128)} %convolution_bitcast_fusion) | data formatting | bytes 12582912 | tf_op jit(solution)/shard_map/reshape | solution.py:178
  152.8 3.3 %convert.9 = bf16[2,3,256,1024]{3,2,1,0:T(8,128)(2,1)S(1)} convert(f32[2,3,256,1024]{3,2,1,0:T(8,128)} %reshape.89) | non-fusion elementwise | flops 1572864 | bytes 9437184 | tf_op jit(solution)/shard_map/convert.4
  166.1 27.7 %all-reduce.3.cloned.1.call-done = f32[2,32,1024]{2,1,0:T(8,128)} async-done(((f32[2,32,1024]{2,1,0:T(8,128)}), f32[2,32,1024]{2,1,0:T(8,128)}) %all-reduce.3.cloned.1.call-update) | async-done | bytes 262160
  194.7 2.8 %fusion.10 = bf16[2,256,1024]{2,1,0:T(8,128)(2,1)S(1)} fusion(f32[2,3,256,1024]{3,2,1,0:T(8,128)} %reshape.89, bf16[2,256,1024]{2,1,0:T(8,128)(2,1)} %collective-permute-done.7, bf16[2,256,1024]{2,1,0:T(8,128)(2,1)} %collective-permute-done.6, f32[2,2,1024]{2,1,0:T(2,128)S(1)} %dynamic-slice_divide_fusion, f32[256]{0:T(256)S(1)} %copy-done.13), kind=kLoop, calls=%fused_computation.20 | loop fusion | flops 3670016 | bytes 5260288 | tf_op jit(solution)/shard_map/convert.2
  (115 shorter events, 41.8 us)
Async XLA Ops:
  7.2 14.5 %copy-start = (bf16[1024,1024]{1,0:T(8,128)(2,1)S(1)}, bf16[1024,1024]{1,0:T(8,128)(2,1)}, u32[]{:S(2)}) copy-start(bf16[1024,1024]{1,0:T(8,128)(2,1)} %param.11) | copy-start | bytes 6291460
  7.2 14.5 %copy-start.16 = (bf16[256,1024]{1,0:T(8,128)(2,1)S(1)}, bf16[256,1024]{1,0:T(8,128)(2,1)}, u32[]{:S(2)}) copy-start(bf16[256,1024]{1,0:T(8,128)(2,1)} %param.10) | copy-start | bytes 1572868
  7.2 186.6 %all-reduce.3.cloned.1.call-start = ((), (), s32[]{:S(2)}) async-start(), calls=%async_computation | async-start | bytes 524288
  9.7 40.5 %collective-permute-start.1 = (bf16[2,256,1024]{2,1,0:T(8,128)(2,1)}, bf16[2,256,1024]{2,1,0:T(8,128)(2,1)}, u32[]{:S(2)}, u32[]{:S(2)}) collective-permute-start(bf16[2,256,1024]{2,1,0:T(8,128)(2,1)} %pad_maximum_fusion.1), channel_id=1, source_target_pairs={{1,0},{2,1},{3,2},{4,3},{5,4},{6,5},{7,6},{8,7},{9,8},{10,9},{11,1... | collective-permute-start | bytes 3145736 | tf_op jit(solution)/shard_map/ppermute | solution.py:36
  15.1 35.1 %collective-permute-start = (bf16[2,256,1024]{2,1,0:T(8,128)(2,1)}, bf16[2,256,1024]{2,1,0:T(8,128)(2,1)}, u32[]{:S(2)}, u32[]{:S(2)}) collective-permute-start(bf16[2,256,1024]{2,1,0:T(8,128)(2,1)} %pad_maximum_fusion.1), channel_id=1, source_target_pairs={{0,1},{1,2},{2,3},{3,4},{4,5},{5,6},{6,7},{7,8},{8,9},{9,10},{10,1... | collective-permute-start | bytes 3145736 | tf_op jit(solution)/shard_map/ppermute | solution.py:34
  18.4 5.8 %copy-start.11 = (f32[2]{0:T(128)}, f32[2]{0:T(128)S(1)}, u32[]{:S(2)}) copy-start(f32[2]{0:T(128)S(1)} %convert_sqrt_fusion) | copy-start | bytes 28
  21.6 17.4 %copy-start.14 = (s32[32,3]{0,1:T(4,128)S(1)}, s32[32,3]{0,1:T(4,128)}, u32[]{:S(2)}) copy-start(s32[32,3]{0,1:T(4,128)} %param.12) | copy-start | bytes 1156
  21.6 2.7 %collective-permute-start.2 = (bf16[1,2,2,1024]{3,2,0,1:T(2,128)(2,1)S(1)}, bf16[1,2,2,1024]{3,2,0,1:T(2,128)(2,1)S(1)}, u32[]{:S(2)}, u32[]{:S(2)}) collective-permute-start(bf16[1,2,2,1024]{3,2,0,1:T(2,128)(2,1)S(1)} %fusion.47), channel_id=1, source_target_pairs={{0,1},{1,0},{2,3},{3,2},{4,5},{5,4},{6,7},{7,6},{8,9},{9,8},{10,11... | collective-permute-start | bytes 24584 | tf_op jit(solution)/shard_map/ppermute | solution.py:20
  22.4 25.5 %copy-start.17 = (u32[32]{0:T(128)S(1)}, u32[32]{0:T(128)}, u32[]{:S(2)}) copy-start(u32[32]{0:T(128)} %constant.62) | copy-start | bytes 388
  22.8 27.2 %copy-start.2 = (bf16[2,128,16,64]{1,0,3,2:T(2,128)(2,1)}, bf16[2,128,16,64]{1,0,3,2:T(2,128)(2,1)S(1)}, u32[]{:S(2)}) copy-start(bf16[2,128,16,64]{1,0,3,2:T(2,128)(2,1)S(1)} %reshape_reshape.7) | copy-start | bytes 1572868
  24.4 12.9 %collective-permute-start.3 = (bf16[2,2,2,1024]{3,2,0,1:T(2,128)(2,1)S(1)}, bf16[2,2,2,1024]{3,2,0,1:T(2,128)(2,1)S(1)}, u32[]{:S(2)}, u32[]{:S(2)}) collective-permute-start(bf16[2,2,2,1024]{3,2,0,1:T(2,128)(2,1)S(1)} %pad_maximum_fusion.6), channel_id=1, source_target_pairs={{0,2},{1,3},{2,0},{3,1},{4,6},{5,7},{6,4},{7,5},{8,10},{9,11},{10,... | collective-permute-start | bytes 49160 | tf_op jit(solution)/shard_map/ppermute | solution.py:20
  37.3 4.0 %collective-permute-start.4 = (bf16[4,2,2,1024]{3,2,0,1:T(2,128)(2,1)S(1)}, bf16[4,2,2,1024]{3,2,0,1:T(2,128)(2,1)S(1)}, u32[]{:S(2)}, u32[]{:S(2)}) collective-permute-start(bf16[4,2,2,1024]{3,2,0,1:T(2,128)(2,1)S(1)} %pad_maximum_fusion.5), channel_id=1, source_target_pairs={{0,4},{1,5},{2,6},{3,7},{4,0},{5,1},{6,2},{7,3},{8,12},{9,13},{10,... | collective-permute-start | bytes 98312 | tf_op jit(solution)/shard_map/ppermute | solution.py:20
  41.5 7.7 %collective-permute-start.5 = (bf16[8,2,2,1024]{3,2,0,1:T(2,128)(2,1)S(1)}, bf16[8,2,2,1024]{3,2,0,1:T(2,128)(2,1)S(1)}, u32[]{:S(2)}, u32[]{:S(2)}) collective-permute-start(bf16[8,2,2,1024]{3,2,0,1:T(2,128)(2,1)S(1)} %pad_maximum_fusion.4), channel_id=1, source_target_pairs={{0,8},{1,9},{2,10},{3,11},{4,12},{5,13},{6,14},{7,15},{8,0},{9,1},... | collective-permute-start | bytes 196616 | tf_op jit(solution)/shard_map/ppermute | solution.py:20
  44.7 38.8 %copy-start.9 = (pred[2,384]{1,0:T(4,128)(4,1)}, pred[2,384]{1,0:T(4,128)(4,1)S(1)}, u32[]{:S(2)}) copy-start(pred[2,384]{1,0:T(4,128)(4,1)S(1)} %broadcast_in_dim.19) | copy-start | bytes 2308
  49.8 35.6 %copy-start.7 = (bf16[32,16,64]{2,1,0:T(8,128)(2,1)}, bf16[32,16,64]{2,1,0:T(8,128)(2,1)S(1)}, u32[]{:S(2)}) copy-start(bf16[32,16,64]{2,1,0:T(8,128)(2,1)S(1)} %reshape_squeeze.15) | copy-start | bytes 196612
  85.0 1.7 copy-start.8
  85.0 1.7 copy-start.10
  127.9 6.6 %copy-start.15 = (s32[6]{0:T(128)S(1)}, s32[6]{0:T(128)}, u32[]{:S(2)}) copy-start(s32[6]{0:T(128)} %eq.35) | copy-start | bytes 76
  156.1 3.5 %copy-start.1 = (bf16[2,384,16,64]{1,3,2,0:T(8,128)(2,1)S(1)}, bf16[2,384,16,64]{1,3,2,0:T(8,128)(2,1)}, u32[]{:S(2)}) copy-start(bf16[2,384,16,64]{1,3,2,0:T(8,128)(2,1)} %reshape_squeeze.13) | copy-start | bytes 4718596
  156.1 3.5 %copy-start.4 = (bf16[2,16,128,384]{2,3,1,0:T(8,128)(2,1)S(1)}, bf16[2,16,128,384]{2,3,1,0:T(8,128)(2,1)}, u32[]{:S(2)}) copy-start(bf16[2,16,128,384]{2,3,1,0:T(8,128)(2,1)} %multiply_convert_fusion) | copy-start | bytes 9437188
  157.6 37.1 %collective-permute-start.6 = (bf16[2,256,1024]{2,1,0:T(8,128)(2,1)}, bf16[2,256,1024]{2,1,0:T(8,128)(2,1)}, u32[]{:S(2)}, u32[]{:S(2)}) collective-permute-start(bf16[2,256,1024]{2,1,0:T(8,128)(2,1)} %get-tuple-element.18), channel_id=1, source_target_pairs={{1,0},{2,1},{3,2},{4,3},{5,4},{6,5},{7,6},{8,7},{9,8},{10,9},{11,1... | collective-permute-start | bytes 3145736 | tf_op jit(solution)/shard_map/ppermute | solution.py:46
  159.3 35.4 %collective-permute-start.7 = (bf16[2,256,1024]{2,1,0:T(8,128)(2,1)}, bf16[2,256,1024]{2,1,0:T(8,128)(2,1)}, u32[]{:S(2)}, u32[]{:S(2)}) collective-permute-start(bf16[2,256,1024]{2,1,0:T(8,128)(2,1)} %get-tuple-element.19), channel_id=1, source_target_pairs={{15,0},{0,1},{1,2},{2,3},{3,4},{4,5},{5,6},{6,7},{7,8},{8,9},{9,10... | collective-permute-start | bytes 3145736 | tf_op jit(solution)/shard_map/ppermute | solution.py:46
  161.2 32.6 %copy-start.12 = (f32[2]{0:T(128)S(1)}, f32[2]{0:T(128)}, u32[]{:S(2)}) copy-start(f32[2]{0:T(128)} %copy-done.11) | copy-start | bytes 28
  161.2 33.5 %copy-start.13 = (f32[256]{0:T(256)S(1)}, f32[256]{0:T(256)}, u32[]{:S(2)}) copy-start(f32[256]{0:T(256)} %get-tuple-element.34) | copy-start | bytes 3076
  (3 other events, 4.6 us)
Sparse Core Ops, SparseCore 0:
  104.0 89.7 all-reduce.2
